TPU v7x, 32 devices: a whole 2x2x4 slice. The times are simulated.
32 devices in a mesh: age: 4 (over z), slab: 8 (over y, x, core).
Axes of the slice: x: 2, y: 2, z: 4, core: 2. Of those that a mesh axis runs over, the one named last changes fastest.
Arguments:
- velocity: float32 [3, 64, 128, 128], P(None, 'age', 'slab'), may hold values from -3 to 3
- mem_lm: float32 [64, 128, 128], P('age', 'slab'), may hold values from -0.5 to 1.5
- mem_mm: float32 [64, 128, 128], P('age', 'slab'), may hold values from 0.5 to 8
- send_ids: int32 [4, 8, 2, 64], P('age', 'slab'), may hold values from -1 to 255, as said below
- read_slot: int32 [4, 64, 128], P(None, 'age', 'slab'), may hold values from 0 to 383, as said below
- weights: float32 [8, 64, 128, 128], P(None, 'age', 'slab'), may hold values from 0 to 1, as said below
Outputs:
- new_lm: float32 [64, 128, 128], P('age', 'slab')
- new_mm: float32 [64, 128, 128], P('age', 'slab')
- viscosity: float32 [64, 128, 128], P('age', 'slab')
Inputs may be any that keep to these rules, and one draw needn't show every extreme that they name: send_ids[g, s, 0] lists in ascending order, followed by -1, the distinct blocks of device (g, s) that the table of device (g, s+1) reads, all in its last 4 columns (j >= 12); send_ids[g, s, 1] likewise for device (g, s-1), all in its first 4 columns. The last device's direction 0 and the first device's direction 1 hold only -1. In every age group some list holds exactly 64 blocks. `read_slot`: A value r names a table line that holds a block: r < 256 an own block, otherwise a slot holding a block id in the list of the device below or above. The corner lines of a cell line are the blocks at rows max(i-1, 0) and max(i-1, 0) + 1 and at two neighbouring cells of the second dimension at most 4 cells away, inside the grid. The eight weights of a cell are the trilinear weights of three fractions, positive and summing to one.
All inputs are finite; a program needn't handle non-finite values.
Results may differ from a plain program's by a relative error of at most 0.0003.
Values sent between devices are 32-bit elements; how exact they have to be, the bound alone decides.
A program may use at most 64 MiB of HBM per device.

v0:
```python
import jax
import jax.numpy as jnp
from jax import lax
from jax.sharding import PartitionSpec as P

pair_list = ((0, 0), (1, 1), (2, 2), (0, 1), (0, 2), (1, 2))
time_step = 0.75
floor_value = 0.3


def extended(block, sides, width):
    for axis, dim in sides:
        count = lax.axis_size(axis)
        forward = [(i, i + 1) for i in range(count - 1)]
        backward = [(target, source) for source, target in forward]
        low = lax.ppermute(
            lax.slice_in_dim(block, block.shape[dim] - width, None, axis=dim), axis, forward
        )
        high = lax.ppermute(lax.slice_in_dim(block, 0, width, axis=dim), axis, backward)
        block = jnp.concatenate([low, block, high], axis=dim)
    return block


def passed_along(block, axis, distance):
    devices = range(lax.axis_size(axis))
    route = [(i - distance, i) for i in devices if i - distance in devices]
    return lax.ppermute(block, axis, route)


def smooth_valid(field):
    along_x = 0.25 * field[:-2] + 0.5 * field[1:-1] + 0.25 * field[2:]
    along_y = 0.25 * along_x[:, :-2] + 0.5 * along_x[:, 1:-1] + 0.25 * along_x[:, 2:]
    return (
        0.25 * jnp.roll(along_y, 1, axis=2) + 0.5 * along_y + 0.25 * jnp.roll(along_y, -1, axis=2)
    )


def magnitude_of(parts):
    total = parts[0] * parts[0] + parts[1] * parts[1] + parts[2] * parts[2]
    total = total + 2.0 * (parts[3] * parts[3] + parts[4] * parts[4] + parts[5] * parts[5])
    return jnp.sqrt(2.0 * total + 1e-06)


def strain_parts(moved):
    along_x = 0.5 * (moved[:, 2:, 1:-1] - moved[:, :-2, 1:-1])
    along_y = 0.5 * (moved[:, 1:-1, 2:] - moved[:, 1:-1, :-2])
    middle = moved[:, 1:-1, 1:-1]
    along_z = 0.5 * (jnp.roll(middle, -1, axis=3) - jnp.roll(middle, 1, axis=3))
    slopes = (along_x, along_y, along_z)
    return [0.5 * (slopes[second][first] + slopes[first][second]) for first, second in pair_list]


def closure(moved, parts, magnitude):
    smooth_u = [smooth_valid(moved[comp]) for comp in range(3)]
    smooth_s = [smooth_valid(part) for part in parts]
    smooth_mag = magnitude_of(smooth_s)
    lm_total = jnp.zeros(smooth_mag.shape, jnp.float32)
    mm_total = jnp.zeros(smooth_mag.shape, jnp.float32)
    for place, (first, second) in enumerate(pair_list):
        factor = 1.0 if first == second else 2.0
        leonard = smooth_valid(moved[first] * moved[second]) - smooth_u[first] * smooth_u[second]
        model = 2.0 * (smooth_valid(magnitude * parts[place]) - 4.0 * smooth_mag * smooth_s[place])
        lm_total = lm_total + factor * leonard * model
        mm_total = mm_total + factor * model * model
    return (lm_total, mm_total)


def corner_sum(picked, corner_weights):
    total = jnp.zeros(corner_weights[..., 0, :, :].shape, jnp.float32)
    for corner in range(8):
        base = picked[..., corner >> 1, :, :]
        if corner & 1:
            base = jnp.roll(base, -1, axis=-1)
        total = total + corner_weights[..., corner, :, :] * base
    return total


def on_device(velocity, mem_lm, mem_mm, send_ids, read_slot, weights):
    rows_x, rows_y, cells_z = mem_lm.shape
    blocks = rows_x * rows_y
    capacity = send_ids.shape[3]
    moved = extended(velocity, (("age", 1), ("slab", 2)), 1)
    own_parts = jnp.stack(strain_parts(moved))
    stacked = extended(own_parts, (("age", 1), ("slab", 2)), 1)
    parts = [stacked[place] for place in range(6)]
    magnitude = magnitude_of(parts)
    lm_local, mm_local = closure(moved, parts, magnitude)
    own_magnitude = magnitude[1:-1, 1:-1]
    lm_rows = mem_lm.reshape(blocks, cells_z)
    mm_rows = mem_mm.reshape(blocks, cells_z)
    corner_rows = read_slot.reshape(4, blocks)
    block_lists = send_ids.reshape(2, capacity)
    valid = (block_lists >= 0)[:, :, None]
    picks = jnp.maximum(block_lists, 0)
    out_lm = jnp.where(valid, lm_rows[picks], 0.0)
    out_mm = jnp.where(valid, mm_rows[picks], 0.0)
    pieces_lm = [lm_rows]
    pieces_mm = [mm_rows]
    for direction, offset in ((0, 1), (1, -1)):
        got_lm, got_mm = passed_along((out_lm[direction], out_mm[direction]), "slab", offset)
        pieces_lm.append(got_lm)
        pieces_mm.append(got_mm)
    table_lm = jnp.concatenate(pieces_lm, axis=0)
    table_mm = jnp.concatenate(pieces_mm, axis=0)
    corner_weights = weights.reshape(8, blocks, cells_z)
    moved_lm = corner_sum(table_lm[corner_rows], corner_weights).reshape(rows_x, rows_y, cells_z)
    moved_mm = corner_sum(table_mm[corner_rows], corner_weights).reshape(rows_x, rows_y, cells_z)
    rate = (
        time_step * jnp.maximum(jnp.maximum(moved_lm, 0.0) * moved_mm, floor_value) ** 0.125 / 1.5
    )
    blend = rate / (1.0 + rate)
    new_lm = jnp.maximum(blend * lm_local + (1.0 - blend) * moved_lm, 0.0)
    new_mm = blend * mm_local + (1.0 - blend) * moved_mm
    viscosity = new_lm / new_mm * own_magnitude
    return (new_lm, new_mm, viscosity)


def solution(mesh):
    return jax.shard_map(
        on_device,
        mesh=mesh,
        in_specs=(
            P(None, "age", "slab", None),
            P("age", "slab", None),
            P("age", "slab", None),
            P("age", "slab", None, None),
            P(None, "age", "slab"),
            P(None, "age", "slab", None),
        ),
        out_specs=(P("age", "slab", None), P("age", "slab", None), P("age", "slab", None)),
        check_vma=False,
    )
```

profile of v0, /device:TPU:12, one launch (start us, length us, event | category | flops | bytes accessed | tf_op | source)
XLA Modules:
  0.0 69.5 jit_solution(2976418717165869518)
XLA Ops:
  0.6 0.8 %fusion.227 = (f32[3,1,16,128]{3,2,1,0:T(8,128)S(1)}, f32[3,1,16,128]{3,2,1,0:T(8,128)S(1)}) fusion(f32[3,16,16,128]{3,2,1,0:T(8,128)} %param.6), kind=kLoop, calls=%fused_computation.458 | loop fusion | bytes 98304 | tf_op jit(solution)/shard_map/slice | solution.py:19
  1.5 3.5 %collective-permute-start.4 = (f32[3,1,16,128]{3,2,1,0:T(8,128)S(1)}, f32[3,1,16,128]{3,2,1,0:T(8,128)S(1)}, u32[]{:S(2)}, u32[]{:S(2)}) collective-permute-start(f32[3,1,16,128]{3,2,1,0:T(8,128)S(1)} %get-tuple-element.72), channel_id=1, source_target_pairs={{0,8},{8,16},{16,24},{1,9},{9,17},{17,25},{2,10},{10,18},{18,26},{... | collective-permute-start | bytes 73736 | tf_op jit(solution)/shard_map/ppermute | solution.py:16
  4.9 2.4 %collective-permute-start.5 = (f32[3,1,16,128]{3,2,1,0:T(8,128)S(1)}, f32[3,1,16,128]{3,2,1,0:T(8,128)S(1)}, u32[]{:S(2)}, u32[]{:S(2)}) collective-permute-start(f32[3,1,16,128]{3,2,1,0:T(8,128)S(1)} %get-tuple-element.71), channel_id=1, source_target_pairs={{8,0},{16,8},{24,16},{9,1},{17,9},{25,17},{10,2},{18,10},{26,18},{... | collective-permute-start | bytes 73736 | tf_op jit(solution)/shard_map/ppermute | solution.py:19
  7.3 0.7 broadcast_maximum_fusion
  8.0 0.7 compare_bitcast_fusion
  8.8 1.5 %gather_fusion = f32[128,128]{1,0:T(8,128)S(1)} fusion(f32[256,128]{1,0:T(8,128)} %bitcast.172, s32[1024]{0:T(1024)S(1)} %pad_clamp_fusion), kind=kCustom, calls=%fused_computation | custom fusion | bytes 131584 | tf_op jit(solution)/shard_map/gather | solution.py:95
  10.3 1.5 %gather_fusion.2 = f32[128,128]{1,0:T(8,128)S(1)} fusion(f32[256,128]{1,0:T(8,128)} %bitcast.170, s32[1024]{0:T(1024)S(1)} %pad_clamp_fusion), kind=kCustom, calls=%fused_computation.2 | custom fusion | bytes 131584 | tf_op jit(solution)/shard_map/gather | solution.py:96
  12.0 2.2 %collective-permute-start.3 = (f32[64,128]{1,0:T(8,128)S(1)}, f32[64,128]{1,0:T(8,128)S(1)}, u32[]{:S(2)}, u32[]{:S(2)}) collective-permute-start(f32[64,128]{1,0:T(8,128)S(1)} %get-tuple-element.165), channel_id=1, source_target_pairs={{1,0},{2,1},{3,2},{4,3},{5,4},{6,5},{7,6},{9,8},{10,9},{11,10},{12... | collective-permute-start | bytes 98312 | tf_op jit(solution)/shard_map/ppermute | solution.py:27
  14.2 2.1 %collective-permute-start.2 = (f32[64,128]{1,0:T(8,128)S(1)}, f32[64,128]{1,0:T(8,128)S(1)}, u32[]{:S(2)}, u32[]{:S(2)}) collective-permute-start(f32[64,128]{1,0:T(8,128)S(1)} %get-tuple-element.164), channel_id=1, source_target_pairs={{0,1},{1,2},{2,3},{3,4},{4,5},{5,6},{6,7},{8,9},{9,10},{10,11},{11... | collective-permute-start | bytes 98312 | tf_op jit(solution)/shard_map/ppermute | solution.py:27
  16.3 0.6 slice_bitcast_fusion.9
  16.9 4.5 %collective-permute-start.1 = (f32[64,128]{1,0:T(8,128)}, f32[64,128]{1,0:T(8,128)}, u32[]{:S(2)}, u32[]{:S(2)}) collective-permute-start(f32[64,128]{1,0:T(8,128)} %get-tuple-element.163), channel_id=1, source_target_pairs={{1,0},{2,1},{3,2},{4,3},{5,4},{6,5},{7,6},{9,8},{10,9},{11,10},{12... | collective-permute-start | bytes 98312 | tf_op jit(solution)/shard_map/ppermute | solution.py:27
  21.4 0.2 fusion.225
  21.6 0.2 fusion.226
  21.9 0.3 fusion.4
  22.2 2.1 %collective-permute-start = (f32[64,128]{1,0:T(8,128)}, f32[64,128]{1,0:T(8,128)}, u32[]{:S(2)}, u32[]{:S(2)}) collective-permute-start(f32[64,128]{1,0:T(8,128)} %get-tuple-element.162), channel_id=1, source_target_pairs={{0,1},{1,2},{2,3},{3,4},{4,5},{5,6},{6,7},{8,9},{9,10},{10,11},{11... | collective-permute-start | bytes 98312 | tf_op jit(solution)/shard_map/ppermute | solution.py:27
  24.4 0.7 fusion.224
  25.1 2.3 %collective-permute-start.6 = (f32[3,18,1,128]{3,2,1,0:T(1,128)}, f32[3,18,1,128]{3,2,1,0:T(1,128)S(1)}, u32[]{:S(2)}, u32[]{:S(2)}) collective-permute-start(f32[3,18,1,128]{3,2,1,0:T(1,128)} %get-tuple-element.64), channel_id=1, source_target_pairs={{0,1},{1,2},{2,3},{3,4},{4,5},{5,6},{6,7},{8,9},{9,10},{10,11},{11... | collective-permute-start | bytes 82952 | tf_op jit(solution)/shard_map/ppermute | solution.py:16
  27.4 4.2 %collective-permute-start.7 = (f32[3,18,1,128]{3,2,1,0:T(1,128)}, f32[3,18,1,128]{3,2,1,0:T(1,128)}, u32[]{:S(2)}, u32[]{:S(2)}) collective-permute-start(f32[3,18,1,128]{3,2,1,0:T(1,128)} %get-tuple-element.63), channel_id=1, source_target_pairs={{1,0},{2,1},{3,2},{4,3},{5,4},{6,5},{7,6},{9,8},{10,9},{11,10},{12... | collective-permute-start | bytes 82952 | tf_op jit(solution)/shard_map/ppermute | solution.py:19
  31.6 2.8 %gather_fusion.3 = f32[1024,128]{1,0:T(8,128)S(1)} fusion(f32[384,128]{1,0:T(8,128)S(1)} %pad_maximum_fusion.7, s32[1024]{0:T(1024)S(1)} %broadcast_clamp_fusion), kind=kCustom, calls=%fused_computation.3 | custom fusion | bytes 1052672 | tf_op jit(solution)/shard_map/gather | solution.py:107
  34.5 0.9 %fusion.222 = (f32[256,127]{1,0:T(8,128)S(1)}, f32[256,127]{1,0:T(8,128)S(1)}, f32[256,127]{1,0:T(8,128)}, f32[256,127]{1,0:T(8,128)}) fusion(f32[1024,128]{1,0:T(8,128)S(1)} %gather_fusion.3), kind=kLoop, calls=%fused_computation.453 | loop fusion | bytes 1040384 | tf_op jit(solution)/shard_map/jit(_roll_static)/slice | solution.py:73
  35.4 0.8 %fusion.221 = (f32[256,128]{1,0:T(8,128)}, f32[256,128]{1,0:T(8,128)}, f32[256,128]{1,0:T(8,128)}, f32[256,128]{1,0:T(8,128)}) fusion(f32[1024,128]{1,0:T(8,128)S(1)} %gather_fusion.3), kind=kLoop, calls=%fused_computation.452 | loop fusion | bytes 1048576 | tf_op jit(solution)/shard_map/slice | solution.py:71
  36.2 0.8 %pad_maximum_fusion.6 = f32[384,128]{1,0:T(8,128)S(1)} fusion(f32[64,128]{1,0:T(8,128)} %collective-permute-done.1, f32[64,128]{1,0:T(8,128)} %collective-permute-done, f32[256,128]{1,0:T(8,128)S(1)} %bitcast.173), kind=kLoop, calls=%fused_computation.149 | loop fusion | flops 98304 | bytes 393216 | tf_op jit(solution)/shard_map/concatenate | solution.py:103
  36.9 2.8 %gather_fusion.1 = f32[1024,128]{1,0:T(8,128)S(1)} fusion(f32[384,128]{1,0:T(8,128)S(1)} %pad_maximum_fusion.6, s32[1024]{0:T(1024)S(1)} %broadcast_clamp_fusion), kind=kCustom, calls=%fused_computation.1 | custom fusion | bytes 1052672 | tf_op jit(solution)/shard_map/gather | solution.py:106
  39.8 0.2 fusion.219
  40.1 0.8 %pad_maximum_fusion.1 = f32[3,18,18,128]{3,2,1,0:T(8,128)S(1)} fusion(f32[3,18,1,128]{3,2,1,0:T(1,128)} %collective-permute-done.7, f32[3,18,16,128]{3,2,1,0:T(8,128)S(1)} %constant_dynamic-update-slice_fusion, f32[3,18,1,128]{3,2,1,0:T(1,128)S(1)} %collective-permute-done.6), kind=kLoop, calls=%fused_computation.5 | loop fusion | flops 248832 | bytes 995328 | tf_op jit(solution)/shard_map/concatenate | solution.py:20
  41.2 0.1 fusion.245
  41.5 0.1 fusion.243
  41.8 0.1 fusion.241
  42.2 0.1 fusion.239
  42.4 0.1 fusion.237
  42.6 0.1 fusion.234
  42.7 0.1 fusion.235
  43.0 0.1 fusion.233
  43.2 0.1 fusion.231
  43.3 0.9 %fusion.1 = f32[3,16,16,128]{3,2,1,0:T(8,128)S(1)} fusion(f32[3,18,16,128]{3,2,1,0:T(8,128)S(1)} %constant_dynamic-update-slice_fusion, f32[3,18,1,128]{3,2,1,0:T(1,128)S(1)} %collective-permute-done.6, f32[3,18,1,128]{3,2,1,0:T(1,128)} %collective-permute-done.7), kind=kLoop, calls=%fused_computation.8 | loop fusion | flops 393216 | bytes 890880 | tf_op jit(solution)/shard_map/mul | solution.py:46
  44.3 1.9 %collective-permute-start.9 = (f32[6,1,16,128]{3,2,1,0:T(8,128)S(1)}, f32[6,1,16,128]{3,2,1,0:T(8,128)S(1)}, u32[]{:S(2)}, u32[]{:S(2)}) collective-permute-start(f32[6,1,16,128]{3,2,1,0:T(8,128)S(1)} %get-tuple-element.29), channel_id=1, source_target_pairs={{8,0},{16,8},{24,16},{9,1},{17,9},{25,17},{10,2},{18,10},{26,18},{... | collective-permute-start | bytes 147464 | tf_op jit(solution)/shard_map/ppermute | solution.py:19
  46.3 3.9 %collective-permute-start.8 = (f32[6,1,16,128]{3,2,1,0:T(8,128)S(1)}, f32[6,1,16,128]{3,2,1,0:T(8,128)S(1)}, u32[]{:S(2)}, u32[]{:S(2)}) collective-permute-start(f32[6,1,16,128]{3,2,1,0:T(8,128)S(1)} %get-tuple-element.28), channel_id=1, source_target_pairs={{0,8},{8,16},{16,24},{1,9},{9,17},{17,25},{2,10},{10,18},{18,26},{... | collective-permute-start | bytes 147464 | tf_op jit(solution)/shard_map/ppermute | solution.py:16
  50.4 1.9 %collective-permute-done.8 = f32[6,1,16,128]{3,2,1,0:T(8,128)S(1)} collective-permute-done((f32[6,1,16,128]{3,2,1,0:T(8,128)S(1)}, f32[6,1,16,128]{3,2,1,0:T(8,128)S(1)}, u32[]{:S(2)}, u32[]{:S(2)}) %collective-permute-start.8) | collective-permute-done | bytes 49184 | tf_op jit(solution)/shard_map/ppermute | solution.py:16
  52.3 1.9 %collective-permute-start.11 = (f32[6,18,1,128]{3,2,1,0:T(1,128)S(1)}, f32[6,18,1,128]{3,2,1,0:T(1,128)S(1)}, u32[]{:S(2)}, u32[]{:S(2)}) collective-permute-start(f32[6,18,1,128]{3,2,1,0:T(1,128)S(1)} %get-tuple-element.27), channel_id=1, source_target_pairs={{1,0},{2,1},{3,2},{4,3},{5,4},{6,5},{7,6},{9,8},{10,9},{11,10},{12... | collective-permute-start | bytes 165896 | tf_op jit(solution)/shard_map/ppermute | solution.py:19
  54.3 2.4 %collective-permute-start.10 = (f32[6,18,1,128]{3,2,1,0:T(1,128)S(1)}, f32[6,18,1,128]{3,2,1,0:T(1,128)S(1)}, u32[]{:S(2)}, u32[]{:S(2)}) collective-permute-start(f32[6,18,1,128]{3,2,1,0:T(1,128)S(1)} %get-tuple-element.26), channel_id=1, source_target_pairs={{0,1},{1,2},{2,3},{3,4},{4,5},{5,6},{6,7},{8,9},{9,10},{10,11},{11... | collective-permute-start | bytes 165896 | tf_op jit(solution)/shard_map/ppermute | solution.py:16
  56.8 3.9 %collective-permute-done.10 = f32[6,18,1,128]{3,2,1,0:T(1,128)S(1)} collective-permute-done((f32[6,18,1,128]{3,2,1,0:T(1,128)S(1)}, f32[6,18,1,128]{3,2,1,0:T(1,128)S(1)}, u32[]{:S(2)}, u32[]{:S(2)}) %collective-permute-start.10) | collective-permute-done | bytes 55328 | tf_op jit(solution)/shard_map/ppermute | solution.py:16
  60.6 0.2 pad_maximum_fusion
  60.9 0.2 fusion.8
  61.0 0.1 fusion.5
  61.3 0.1 fusion.247
  61.6 0.1 fusion.267
  61.7 0.2 fusion.43
  62.1 0.1 fusion.263
  62.2 0.1 fusion.260
  62.3 0.1 fusion.261
  62.6 0.1 fusion.259
  62.9 0.1 fusion.257
  63.0 0.1 fusion.254
  63.1 0.1 fusion.255
  63.2 0.1 fusion.265
  63.3 0.1 fusion.264
  63.6 0.1 fusion.252
  63.9 0.1 fusion.268
  64.4 0.1 fusion.250
  64.5 0.7 %fusion.193 = (f32[16,16,128]{2,1,0:T(8,128)S(1)}, f32[16,16,128]{2,1,0:T(8,128)S(1)}, f32[16,16,128]{2,1,0:T(8,128)S(1)}, f32[16,16,128]{2,1,0:T(8,128)S(1)}, f...) fusion(f32[16,16,127]{2,1,0:T(8,128)S(1)} %get-tuple-element.155, ...), kind=kLoop, calls=%fused_computation.394 | loop fusion | flops 2326528 | bytes 3932160 | tf_op jit(solution)/shard_map/sub | solution.py:62
  65.3 0.3 fusion.175
  65.6 0.3 fusion.153
  66.0 0.8 %copy-done.3 = f32[8,16,16,128]{3,2,1,0:T(8,128)S(1)} copy-done((f32[8,16,16,128]{3,2,1,0:T(8,128)S(1)}, f32[8,16,16,128]{3,2,1,0:T(8,128)}, u32[]{:S(2)}) %copy-start.3) | copy-done | bytes 1048600
  66.9 2.5 %slice_multiply_fusion.69 = (f32[16,16,128]{2,1,0:T(8,128)}, f32[16,16,128]{2,1,0:T(8,128)}, f32[16,16,128]{2,1,0:T(8,128)}) fusion(f32[18,18,128]{2,1,0:T(8,128)S(1)} %get-tuple-element.14, f32[16,16,128]{2,1,0:T(8,128)S(1)} %get-tuple-element.111, f32[16,16,128]{2,1,0:T(8,128)S(1)} %get-tuple-element.110, f32[16,16,128]{2,1,0:T(8,128)S(1)} %get-tuple-element.6, ...), kind=kLoop, calls=%fused_computation.158 | loop fusion | flops 6389760 | bytes 9830400 | tf_op jit(solution)/shard_map/mul | solution.py:114
  (99 shorter events, 4.1 us)
Async XLA Ops:
  0.6 20.8 %copy-start = (f32[3,16,16,128]{3,2,1,0:T(8,128)S(1)}, f32[3,16,16,128]{3,2,1,0:T(8,128)}, u32[]{:S(2)}) copy-start(f32[3,16,16,128]{3,2,1,0:T(8,128)} %param.6) | copy-start | bytes 1179652
  1.5 20.8 %collective-permute-start.4 = (f32[3,1,16,128]{3,2,1,0:T(8,128)S(1)}, f32[3,1,16,128]{3,2,1,0:T(8,128)S(1)}, u32[]{:S(2)}, u32[]{:S(2)}) collective-permute-start(f32[3,1,16,128]{3,2,1,0:T(8,128)S(1)} %get-tuple-element.72), channel_id=1, source_target_pairs={{0,8},{8,16},{16,24},{1,9},{9,17},{17,25},{2,10},{10,18},{18,26},{... | collective-permute-start | bytes 73736 | tf_op jit(solution)/shard_map/ppermute | solution.py:16
  4.9 19.4 %collective-permute-start.5 = (f32[3,1,16,128]{3,2,1,0:T(8,128)S(1)}, f32[3,1,16,128]{3,2,1,0:T(8,128)S(1)}, u32[]{:S(2)}, u32[]{:S(2)}) collective-permute-start(f32[3,1,16,128]{3,2,1,0:T(8,128)S(1)} %get-tuple-element.71), channel_id=1, source_target_pairs={{8,0},{16,8},{24,16},{9,1},{17,9},{25,17},{10,2},{18,10},{26,18},{... | collective-permute-start | bytes 73736 | tf_op jit(solution)/shard_map/ppermute | solution.py:19
  12.0 15.4 %collective-permute-start.3 = (f32[64,128]{1,0:T(8,128)S(1)}, f32[64,128]{1,0:T(8,128)S(1)}, u32[]{:S(2)}, u32[]{:S(2)}) collective-permute-start(f32[64,128]{1,0:T(8,128)S(1)} %get-tuple-element.165), channel_id=1, source_target_pairs={{1,0},{2,1},{3,2},{4,3},{5,4},{6,5},{7,6},{9,8},{10,9},{11,10},{12... | collective-permute-start | bytes 98312 | tf_op jit(solution)/shard_map/ppermute | solution.py:27
  14.2 17.4 %collective-permute-start.2 = (f32[64,128]{1,0:T(8,128)S(1)}, f32[64,128]{1,0:T(8,128)S(1)}, u32[]{:S(2)}, u32[]{:S(2)}) collective-permute-start(f32[64,128]{1,0:T(8,128)S(1)} %get-tuple-element.164), channel_id=1, source_target_pairs={{0,1},{1,2},{2,3},{3,4},{4,5},{5,6},{6,7},{8,9},{9,10},{10,11},{11... | collective-permute-start | bytes 98312 | tf_op jit(solution)/shard_map/ppermute | solution.py:27
  16.9 4.9 %copy-start.10 = (s32[4,16,16]{2,1,0:T(8,128)S(1)}, s32[4,16,16]{2,1,0:T(8,128)}, u32[]{:S(2)}) copy-start(s32[4,16,16]{2,1,0:T(8,128)} %param.10) | copy-start | bytes 12292
  16.9 19.2 %collective-permute-start.1 = (f32[64,128]{1,0:T(8,128)}, f32[64,128]{1,0:T(8,128)}, u32[]{:S(2)}, u32[]{:S(2)}) collective-permute-start(f32[64,128]{1,0:T(8,128)} %get-tuple-element.163), channel_id=1, source_target_pairs={{1,0},{2,1},{3,2},{4,3},{5,4},{6,5},{7,6},{9,8},{10,9},{11,10},{12... | collective-permute-start | bytes 98312 | tf_op jit(solution)/shard_map/ppermute | solution.py:27
  22.2 9.4 %copy-start.1 = (f32[16,16,128]{2,1,0:T(8,128)S(1)}, f32[16,16,128]{2,1,0:T(8,128)}, u32[]{:S(2)}) copy-start(f32[16,16,128]{2,1,0:T(8,128)} %param.8) | copy-start | bytes 393220
  22.2 13.9 %collective-permute-start = (f32[64,128]{1,0:T(8,128)}, f32[64,128]{1,0:T(8,128)}, u32[]{:S(2)}, u32[]{:S(2)}) collective-permute-start(f32[64,128]{1,0:T(8,128)} %get-tuple-element.162), channel_id=1, source_target_pairs={{0,1},{1,2},{2,3},{3,4},{4,5},{5,6},{6,7},{8,9},{9,10},{10,11},{11... | collective-permute-start | bytes 98312 | tf_op jit(solution)/shard_map/ppermute | solution.py:27
  25.1 15.0 %collective-permute-start.6 = (f32[3,18,1,128]{3,2,1,0:T(1,128)}, f32[3,18,1,128]{3,2,1,0:T(1,128)S(1)}, u32[]{:S(2)}, u32[]{:S(2)}) collective-permute-start(f32[3,18,1,128]{3,2,1,0:T(1,128)} %get-tuple-element.64), channel_id=1, source_target_pairs={{0,1},{1,2},{2,3},{3,4},{4,5},{5,6},{6,7},{8,9},{9,10},{10,11},{11... | collective-permute-start | bytes 82952 | tf_op jit(solution)/shard_map/ppermute | solution.py:16
  27.4 12.7 %collective-permute-start.7 = (f32[3,18,1,128]{3,2,1,0:T(1,128)}, f32[3,18,1,128]{3,2,1,0:T(1,128)}, u32[]{:S(2)}, u32[]{:S(2)}) collective-permute-start(f32[3,18,1,128]{3,2,1,0:T(1,128)} %get-tuple-element.63), channel_id=1, source_target_pairs={{1,0},{2,1},{3,2},{4,3},{5,4},{6,5},{7,6},{9,8},{10,9},{11,10},{12... | collective-permute-start | bytes 82952 | tf_op jit(solution)/shard_map/ppermute | solution.py:19
  34.4 1.7 %copy-start.2 = (f32[16,16,128]{2,1,0:T(8,128)S(1)}, f32[16,16,128]{2,1,0:T(8,128)}, u32[]{:S(2)}) copy-start(f32[16,16,128]{2,1,0:T(8,128)} %param.7) | copy-start | bytes 393220
  44.3 6.0 %collective-permute-start.9 = (f32[6,1,16,128]{3,2,1,0:T(8,128)S(1)}, f32[6,1,16,128]{3,2,1,0:T(8,128)S(1)}, u32[]{:S(2)}, u32[]{:S(2)}) collective-permute-start(f32[6,1,16,128]{3,2,1,0:T(8,128)S(1)} %get-tuple-element.29), channel_id=1, source_target_pairs={{8,0},{16,8},{24,16},{9,1},{17,9},{25,17},{10,2},{18,10},{26,18},{... | collective-permute-start | bytes 147464 | tf_op jit(solution)/shard_map/ppermute | solution.py:19
  46.3 6.0 %collective-permute-start.8 = (f32[6,1,16,128]{3,2,1,0:T(8,128)S(1)}, f32[6,1,16,128]{3,2,1,0:T(8,128)S(1)}, u32[]{:S(2)}, u32[]{:S(2)}) collective-permute-start(f32[6,1,16,128]{3,2,1,0:T(8,128)S(1)} %get-tuple-element.28), channel_id=1, source_target_pairs={{0,8},{8,16},{16,24},{1,9},{9,17},{17,25},{2,10},{10,18},{18,26},{... | collective-permute-start | bytes 147464 | tf_op jit(solution)/shard_map/ppermute | solution.py:16
  52.3 4.4 %collective-permute-start.11 = (f32[6,18,1,128]{3,2,1,0:T(1,128)S(1)}, f32[6,18,1,128]{3,2,1,0:T(1,128)S(1)}, u32[]{:S(2)}, u32[]{:S(2)}) collective-permute-start(f32[6,18,1,128]{3,2,1,0:T(1,128)S(1)} %get-tuple-element.27), channel_id=1, source_target_pairs={{1,0},{2,1},{3,2},{4,3},{5,4},{6,5},{7,6},{9,8},{10,9},{11,10},{12... | collective-permute-start | bytes 165896 | tf_op jit(solution)/shard_map/ppermute | solution.py:19
  54.3 6.4 %collective-permute-start.10 = (f32[6,18,1,128]{3,2,1,0:T(1,128)S(1)}, f32[6,18,1,128]{3,2,1,0:T(1,128)S(1)}, u32[]{:S(2)}, u32[]{:S(2)}) collective-permute-start(f32[6,18,1,128]{3,2,1,0:T(1,128)S(1)} %get-tuple-element.26), channel_id=1, source_target_pairs={{0,1},{1,2},{2,3},{3,4},{4,5},{5,6},{6,7},{8,9},{9,10},{10,11},{11... | collective-permute-start | bytes 165896 | tf_op jit(solution)/shard_map/ppermute | solution.py:16
  65.5 1.2 %copy-start.3 = (f32[8,16,16,128]{3,2,1,0:T(8,128)S(1)}, f32[8,16,16,128]{3,2,1,0:T(8,128)}, u32[]{:S(2)}) copy-start(f32[8,16,16,128]{3,2,1,0:T(8,128)} %param.11) | copy-start | bytes 3145732
  65.5 1.2 %copy-start.4 = (f32[256,127]{1,0:T(8,128)S(1)}, f32[256,127]{1,0:T(8,128)}, u32[]{:S(2)}) copy-start(f32[256,127]{1,0:T(8,128)} %get-tuple-element.57) | copy-start | bytes 390148
  65.5 1.2 %copy-start.5 = (f32[256,127]{1,0:T(8,128)S(1)}, f32[256,127]{1,0:T(8,128)}, u32[]{:S(2)}) copy-start(f32[256,127]{1,0:T(8,128)} %get-tuple-element.58) | copy-start | bytes 390148
  65.6 1.3 %copy-start.6 = (f32[256,128]{1,0:T(8,128)S(1)}, f32[256,128]{1,0:T(8,128)}, u32[]{:S(2)}) copy-start(f32[256,128]{1,0:T(8,128)} %get-tuple-element.51) | copy-start | bytes 393220
  65.6 1.3 %copy-start.7 = (f32[256,128]{1,0:T(8,128)S(1)}, f32[256,128]{1,0:T(8,128)}, u32[]{:S(2)}) copy-start(f32[256,128]{1,0:T(8,128)} %get-tuple-element.52) | copy-start | bytes 393220
  65.6 1.3 %copy-start.8 = (f32[256,128]{1,0:T(8,128)S(1)}, f32[256,128]{1,0:T(8,128)}, u32[]{:S(2)}) copy-start(f32[256,128]{1,0:T(8,128)} %get-tuple-element.53) | copy-start | bytes 393220
  65.6 1.4 %copy-start.9 = (f32[256,128]{1,0:T(8,128)S(1)}, f32[256,128]{1,0:T(8,128)}, u32[]{:S(2)}) copy-start(f32[256,128]{1,0:T(8,128)} %get-tuple-element.54) | copy-start | bytes 393220
where the time goes:
time: 70.7 us; the launch traced here: 69.5 us
  starting transfers between devices  33.3 us (47%)
  local copies, waits for them, and re-layouts  18.3 us (26%)
  other arithmetic  10.4 us (15%)
  waiting for transfers between devices  5.77 us (8%)
  between operations  1.61 us (2%)
    ppermute x4, starting transfers between devices, extended(): lax.ppermute(lax.slice_in_dim(block, block.shape[dim] - width, None, axis...  12.1 us
    ppermute x4, starting transfers between devices, passed_along(): return lax.ppermute(block, axis, route)  10.9 us
    ppermute x4, starting transfers between devices, extended(): lax.ppermute(lax.slice_in_dim(block, 0, width, axis=dim), axis, backward)  10.4 us
    ppermute x4, waiting for transfers between devices, extended(): lax.ppermute(lax.slice_in_dim(block, block.shape[dim] - width, None, axis...  5.75 us
    gather x1, local copies, waits for them, and re-layouts, on_device(): table_mm[corner_rows]  2.81 us
    gather x1, local copies, waits for them, and re-layouts, on_device(): table_lm[corner_rows]  2.81 us
    slice x28, local copies, waits for them, and re-layouts, smooth_valid(): jnp.roll(along_y, 1, axis=2)  2.62 us
    mul x1, other arithmetic, on_device(): viscosity = new_lm / new_mm * own_magnitude  2.51 us
  transfers between devices with their start and end apart: 12, of which 2 were waited for; matrix products, arithmetic and copies ran while one was open for 22% of the time, Pallas kernels for 0%

commit v1 on v0

v1 whole, which is shorter than its diff:
```python
import functools

import jax
import jax.numpy as jnp
from jax import lax
from jax.experimental import pallas as pl
from jax.experimental.pallas import tpu as pltpu
from jax.sharding import PartitionSpec as P

pair_list = ((0, 0), (1, 1), (2, 2), (0, 1), (0, 2), (1, 2))
time_step = 0.75
floor_value = 0.3
directions = tuple((dx, dy) for dx in (-1, 0, 1) for dy in (-1, 0, 1) if (dx, dy) != (0, 0))
reach = 4
pad_y = 8
MESH = pl.DeviceIdType.MESH


def halves(table):
    high = table.astype(jnp.bfloat16)
    low = (table - high.astype(jnp.float32)).astype(jnp.bfloat16)
    return jnp.concatenate([high, low], axis=0)


def root(value):
    return value * lax.rsqrt(value)


def kernel(
    vel, lm_in, mm_in, ids, slots_in, weights_in, out_lm, out_mm, out_visc,
    u, lm, mm, slots, w, raw, lists, picked, raws, mags, smooth,
    send_sems, recv_sems, local_sems,
):
    nx, ny, nz = lm.shape
    groups, peers = lax.axis_size("age"), lax.axis_size("slab")
    g, s = lax.axis_index("age"), lax.axis_index("slab")

    def has(dx, dy):
        ok = jnp.bool_(True)
        if dx < 0:
            ok = ok & (g > 0)
        if dx > 0:
            ok = ok & (g < groups - 1)
        if dy < 0:
            ok = ok & (s > 0)
        if dy > 0:
            ok = ok & (s < peers - 1)
        return ok

    own_vel = pltpu.make_async_copy(
        vel, u.at[:, pl.ds(2, nx), pl.ds(pad_y, ny), :], local_sems.at[0]
    )
    own_copies = [
        pltpu.make_async_copy(slots_in, slots, local_sems.at[1]),
        pltpu.make_async_copy(lm_in, lm, local_sems.at[2]),
        pltpu.make_async_copy(mm_in, mm, local_sems.at[3]),
    ]
    weight_copy = pltpu.make_async_copy(weights_in, w, local_sems.at[4])

    barrier = pltpu.get_barrier_semaphore()
    for dx, dy in directions:
        @pl.when(has(dx, dy))
        def _(dx=dx, dy=dy):
            pl.semaphore_signal(barrier, inc=1, device_id=(g + dx, s + dy), device_id_type=MESH)

    for copy in own_copies:
        copy.start()
    own_vel.start()
    weight_copy.start()

    zero = jnp.zeros((), jnp.float32)
    for dx, place in ((-1, 0), (1, nx + 2)):
        @pl.when(jnp.logical_not(has(dx, 0)))
        def _(place=place):
            u[:, place : place + 2, :, :] = jnp.zeros((3, 2) + u.shape[2:], jnp.float32)
    for dy, place in ((-1, pad_y - 2), (1, pad_y + ny)):
        @pl.when(jnp.logical_not(has(0, dy)))
        def _(dy=dy, place=place):
            u[:, :, place : place + 2, :] = jnp.zeros(u.shape[:2] + (2, nz), jnp.float32)
            side = 0 if dy < 0 else 1
            raw[:, :, side * reach : (side + 1) * reach, :] = jnp.zeros((2, nx, reach, nz), jnp.float32)
            lists[side] = jnp.full(lists.shape[1:], -1, jnp.int32)

    def span(step, cells, begin):
        if step == 0:
            return pl.ds(0, cells), pl.ds(begin, cells)
        if step > 0:
            return pl.ds(cells - 2, 2), pl.ds(begin - 2, 2)
        return pl.ds(0, 2), pl.ds(begin + cells, 2)

    def remote(source, target, place, dx, dy):
        return pltpu.make_async_remote_copy(
            src_ref=source, dst_ref=target, send_sem=send_sems.at[place],
            recv_sem=recv_sems.at[place], device_id=(g + dx, s + dy), device_id_type=MESH,
        )

    halo = []
    for place, (dx, dy) in enumerate(directions):
        from_x, to_x = span(dx, nx, 2)
        from_y, to_y = span(dy, ny, pad_y)
        halo.append((
            dx, dy,
            remote(vel.at[:, from_x, from_y, :], u.at[:, to_x, to_y, :], place, dx, dy),
        ))
    memory = []
    place = len(directions)
    for dy in (1, -1):
        side = 0 if dy > 0 else 1
        columns = pl.ds(ny - reach, reach) if dy > 0 else pl.ds(0, reach)
        for number, field in enumerate((lm_in, mm_in)):
            memory.append((0, dy, remote(
                field.at[:, columns, :], raw.at[number, :, pl.ds(side * reach, reach), :], place, 0, dy
            )))
            place += 1
        memory.append((0, dy, remote(ids.at[0, 0], lists.at[side], place, 0, dy)))
        place += 1

    incoming = (
        ((g > 0).astype(jnp.int32) + (g < groups - 1).astype(jnp.int32) + 1)
        * ((s > 0).astype(jnp.int32) + (s < peers - 1).astype(jnp.int32) + 1)
        - 1
    )
    pl.semaphore_wait(barrier, incoming)
    for dx, dy, copy in halo + memory:
        @pl.when(has(dx, dy))
        def _(copy=copy):
            copy.start()

    for copy in own_copies:
        copy.wait()
    lines = 4 * nx
    blocks = nx * ny
    eye = lax.broadcasted_iota(jnp.int32, (1, ny, ny), 1) == lax.broadcasted_iota(jnp.int32, (1, ny, ny), 2)
    slot_rows = slots[...].astype(jnp.float32).reshape(lines, 1, ny)
    slot_column = jnp.sum(jnp.where(eye, slot_rows, 0.0), axis=2, keepdims=True)

    def one_hot(begin, count):
        ids_of = (lax.broadcasted_iota(jnp.int32, (1, 1, count), 2) + begin).astype(jnp.float32)
        hot = jnp.where(slot_column == ids_of, 1.0, 0.0)
        hot = hot.reshape(lines * ny, count).astype(jnp.bfloat16)
        return jnp.concatenate([hot, hot], axis=1)

    own_table = jnp.concatenate([lm[...].reshape(blocks, nz), mm[...].reshape(blocks, nz)], axis=1)
    picked[...] = jnp.dot(one_hot(0, blocks), halves(own_table), preferred_element_type=jnp.float32)

    own_vel.wait()
    for dx, dy, copy in halo:
        @pl.when(has(-dx, -dy))
        def _(copy=copy):
            copy.wait_recv()

    rows = raws.shape[1]
    row = lax.broadcasted_iota(jnp.int32, (rows, nz), 0)
    inside_low = jnp.where((row > 0) | (s > 0), 1.0, 0.0)
    inside = jnp.where((row < ny + 1) | (s < peers - 1), inside_low, 0.0)

    def strain_step(e, carry):
        shift = e // 1024
        def get(comp, along_x, along_y, count=rows):
            return u[comp, e + 1 + along_x, pl.ds(pad_y - 1 + along_y + shift, count), :]
        center = [get(comp, 0, 0) for comp in range(3)]
        slopes = [
            [get(comp, 1, 0) - get(comp, -1, 0) for comp in range(3)],
            [get(comp, 0, 1) - get(comp, 0, -1) for comp in range(3)],
            [pltpu.roll(center[comp], nz - 1, 1) - pltpu.roll(center[comp], 1, 1) for comp in range(3)],
        ]
        within = jnp.where(((e > 0) | (g > 0)) & ((e < nx + 1) | (g < groups - 1)), 1.0, 0.0)
        mask = inside * within
        parts = [(slopes[b][a] + slopes[a][b]) * mask for a, b in pair_list]
        total = parts[0] * parts[0] + parts[1] * parts[1] + parts[2] * parts[2]
        total = total + 2.0 * (parts[3] * parts[3] + parts[4] * parts[4] + parts[5] * parts[5])
        mag = root(total * 0.125 + 1e-06)
        mags[e] = mag
        for place in range(6):
            a, b = pair_list[place]
            raws[place] = parts[place]
            raws[6 + place] = mag * parts[place]
            raws[12 + place] = center[a] * center[b]
        for place in range(18):
            below = raws[place, pl.ds(shift, ny), :]
            middle = raws[place, pl.ds(shift + 1, ny), :]
            above = raws[place, pl.ds(shift + 2, ny), :]
            smooth[place, e] = (below + above) + (middle + middle)
        for comp in range(3):
            middle = get(comp, 0, 1, ny)
            smooth[18 + comp, e] = (get(comp, 0, 0, ny) + get(comp, 0, 2, ny)) + (middle + middle)
        return carry

    lax.fori_loop(0, nx + 2, strain_step, 0)

    for dx, dy, copy in memory:
        @pl.when(has(-dx, -dy))
        def _(copy=copy):
            copy.wait_recv()
    strip = nx * 2 * reach
    near = jnp.concatenate([raw[0].reshape(strip, nz), raw[1].reshape(strip, nz)], axis=1)
    near = halves(near)
    capacity = lists.shape[2]
    line = lax.broadcasted_iota(jnp.int32, (strip, capacity), 0)
    column = line % (2 * reach)
    line_row = line // (2 * reach)
    below_id = jnp.where(column < reach, line_row * ny + (ny - reach) + column, -5)
    above_id = jnp.where(column >= reach, line_row * ny + column - reach, -5)
    listed = []
    for side, block_id in ((0, below_id), (1, above_id)):
        hot = jnp.where(block_id == lists[side, side : side + 1, :], 1.0, 0.0).astype(jnp.bfloat16)
        hot = jnp.concatenate([hot, hot], axis=0)
        listed.append(lax.dot_general(hot, near, (((0,), (0,)), ((), ())), preferred_element_type=jnp.float32))
    far_table = halves(jnp.concatenate(listed, axis=0))
    picked[...] += jnp.dot(one_hot(blocks, 2 * capacity), far_table, preferred_element_type=jnp.float32)
    weight_copy.wait()

    def final_step(x, carry):
        shift = x // 1024
        def filtered(place):
            f = (smooth[place, x] + smooth[place, x + 2]) + 2.0 * smooth[place, x + 1]
            f = f + pltpu.roll(f, 1, 1)
            return f + pltpu.roll(f, nz - 1, 1)
        flow = [0.125 * filtered(18 + comp) for comp in range(3)]
        parts = [filtered(place) for place in range(6)]
        total = parts[0] * parts[0] + parts[1] * parts[1] + parts[2] * parts[2]
        total = total + 2.0 * (parts[3] * parts[3] + parts[4] * parts[4] + parts[5] * parts[5])
        mag4 = 4.0 * root(total * (2.0 / 65536.0) + 1e-06)
        lm_sum, mm_sum = [], []
        for half in (range(3), range(3, 6)):
            lm_part = mm_part = None
            for place in half:
                a, b = pair_list[place]
                leonard = filtered(12 + place) - flow[a] * flow[b]
                model = filtered(6 + place) - mag4 * parts[place]
                lm_part = leonard * model if lm_part is None else lm_part + leonard * model
                mm_part = model * model if mm_part is None else mm_part + model * model
            lm_sum.append(lm_part)
            mm_sum.append(mm_part)
        lm_local = (lm_sum[0] + 2.0 * lm_sum[1]) * (1.0 / 8192.0)
        mm_local = (mm_sum[0] + 2.0 * mm_sum[1]) * (1.0 / 16384.0)
        moved = [None, None]
        for corner in range(4):
            low, high = w[2 * corner, x], w[2 * corner + 1, x]
            start = pl.multiple_of((corner * nx + x) * ny, ny)
            for field in range(2):
                base = picked[pl.ds(start, ny), field * nz : (field + 1) * nz]
                term = low * base + high * pltpu.roll(base, nz - 1, 1)
                moved[field] = term if moved[field] is None else moved[field] + term
        moved_lm, moved_mm = moved
        power = root(root(root(jnp.maximum(jnp.maximum(moved_lm, 0.0) * moved_mm, floor_value))))
        rate = (time_step / 1.5) * power
        blend = rate / (1.0 + rate)
        new_lm = jnp.maximum(moved_lm + blend * (lm_local - moved_lm), 0.0)
        new_mm = moved_mm + blend * (mm_local - moved_mm)
        out_lm[x] = new_lm
        out_mm[x] = new_mm
        out_visc[x] = new_lm / new_mm * mags[x + 1, pl.ds(1 + shift, ny), :]
        return carry

    lax.fori_loop(0, nx, final_step, 0)

    for dx, dy, copy in halo + memory:
        @pl.when(has(dx, dy))
        def _(copy=copy):
            copy.wait_send()


def on_device(velocity, mem_lm, mem_mm, send_ids, read_slot, weights):
    nx, ny, nz = mem_lm.shape
    capacity = send_ids.shape[3]
    f32 = jnp.float32
    rows = ny + 8
    out = jax.ShapeDtypeStruct(mem_lm.shape, f32)
    copies = len(directions) + 6
    return pl.pallas_call(
        kernel,
        out_shape=(out, out, out),
        in_specs=[pl.BlockSpec(memory_space=pl.ANY)] * 6,
        out_specs=[pl.BlockSpec(memory_space=pltpu.VMEM)] * 3,
        scratch_shapes=[
            pltpu.VMEM((3, nx + 4, ny + 2 * pad_y, nz), f32),
            pltpu.VMEM(mem_lm.shape, f32),
            pltpu.VMEM(mem_lm.shape, f32),
            pltpu.VMEM(read_slot.shape, jnp.int32),
            pltpu.VMEM(weights.shape, f32),
            pltpu.VMEM((2, nx, 2 * reach, nz), f32),
            pltpu.VMEM((2, 2, capacity), jnp.int32),
            pltpu.VMEM((4 * nx * ny, 2 * nz), f32),
            pltpu.VMEM((18, rows, nz), f32),
            pltpu.VMEM((nx + 2, rows, nz), f32),
            pltpu.VMEM((21, nx + 2, ny, nz), f32),
            pltpu.SemaphoreType.DMA((copies,)),
            pltpu.SemaphoreType.DMA((copies,)),
            pltpu.SemaphoreType.DMA((5,)),
        ],
        compiler_params=pltpu.CompilerParams(
            collective_id=0, has_side_effects=True, vmem_limit_bytes=48 << 20
        ),
    )(velocity, mem_lm, mem_mm, send_ids, read_slot, weights)


def solution(mesh):
    return jax.shard_map(
        on_device,
        mesh=mesh,
        in_specs=(
            P(None, "age", "slab", None),
            P("age", "slab", None),
            P("age", "slab", None),
            P("age", "slab", None, None),
            P(None, "age", "slab"),
            P(None, "age", "slab", None),
        ),
        out_specs=(P("age", "slab", None), P("age", "slab", None), P("age", "slab", None)),
        check_vma=False,
    )
```

time: 70.7 us -> 22.1 us (0.31); the launches traced: 69.5 us -> 21.7 us
  starting transfers between devices: 33.3 us -> 0 us
  Pallas kernels: 0 us -> 13.7 us
  local copies, waits for them, and re-layouts: 18.3 us -> 7.42 us
  other arithmetic: 10.4 us -> 0 us
  waiting for transfers between devices: 5.77 us -> 0 us
  between operations: 1.61 us -> 0.65 us
    ppermute x12 -> x0, starting transfers between devices: 33.3 us -> none  [the longest x4 12.1 us: extended(): lax.ppermute(lax.slice_in_dim(block, block.shape[dim] - width, None, axis...]
    pallas_call x0 -> x1, Pallas kernels: none -> 13.7 us  [on_device(): pl.pallas_call(kernel, out_shape=(out, out, out), in_specs=[pl.BlockSpec(...]
    gather x4 -> x0, local copies, waits for them, and re-layouts: 8.71 us -> none  [the longest x1 2.81 us: on_device(): table_mm[corner_rows]]
    slice x53 -> x0, local copies, waits for them, and re-layouts: 7.76 us -> none  [the longest x28 2.62 us: smooth_valid(): jnp.roll(along_y, 1, axis=2)]
    unnamed x24 -> x15, local copies, waits for them, and re-layouts: 1.05 us -> 7.42 us
    ppermute x12 -> x0, waiting for transfers between devices: 5.77 us -> none  [the longest x4 5.75 us: extended(): lax.ppermute(lax.slice_in_dim(block, block.shape[dim] - width, None, axis...]
    mul x8 -> x0, other arithmetic: 4.61 us -> none  [the longest x1 2.51 us: on_device(): viscosity = new_lm / new_mm * own_magnitude]
    concatenate x4 -> x0, other arithmetic: 1.86 us -> none  [the longest x2 1.06 us: extended(): block = jnp.concatenate([low, block, high], axis=dim)]
  transfers between devices with their start and end apart: 12 -> 0, of which waited for: 2 -> 0; matrix products, arithmetic and copies ran while one was open for 22% -> 0% of each run, Pallas kernels for 0% -> 0%
where the time goes in v1:
time: 22.1 us; the launch traced here: 21.7 us
  Pallas kernels  13.7 us (62%)
  local copies, waits for them, and re-layouts  7.42 us (34%)
  between operations  0.65 us (3%)
    pallas_call x1, Pallas kernels, on_device(): pl.pallas_call(kernel, out_shape=(out, out, out), in_specs=[pl.BlockSpec(...  13.7 us
    unnamed x15, local copies, waits for them, and re-layouts  7.42 us

profile of v1, /device:TPU:12, one launch (start us, length us, event | category | flops | bytes accessed | tf_op | source)
XLA Modules:
  0.0 21.7 jit_solution(13811108751680666894)
XLA Ops:
  0.6 0.0 copy-start
  0.6 1.2 %copy-done = f32[8,16,16,128]{3,2,1,0:T(8,128)S(1)} copy-done((f32[8,16,16,128]{3,2,1,0:T(8,128)S(1)}, f32[8,16,16,128]{3,2,1,0:T(8,128)}, u32[]{:S(2)}) %copy-start) | copy-done | bytes 1048600
  1.9 0.0 copy-start.1
  1.9 1.0 %copy-done.1 = f32[3,16,16,128]{3,2,1,0:T(8,128)S(1)} copy-done((f32[3,16,16,128]{3,2,1,0:T(8,128)S(1)}, f32[3,16,16,128]{3,2,1,0:T(8,128)}, u32[]{:S(2)}) %copy-start.1) | copy-done | bytes 393240
  2.9 0.0 copy-start.2
  2.9 0.9 %copy-done.2 = f32[16,16,128]{2,1,0:T(8,128)S(1)} copy-done((f32[16,16,128]{2,1,0:T(8,128)S(1)}, f32[16,16,128]{2,1,0:T(8,128)}, u32[]{:S(2)}) %copy-start.2) | copy-done | bytes 131096
  3.8 0.0 copy-start.3
  3.8 0.9 %copy-done.3 = f32[16,16,128]{2,1,0:T(8,128)S(1)} copy-done((f32[16,16,128]{2,1,0:T(8,128)S(1)}, f32[16,16,128]{2,1,0:T(8,128)}, u32[]{:S(2)}) %copy-start.3) | copy-done | bytes 131096
  4.7 0.0 copy-start.4
  4.7 0.8 %copy-done.4 = s32[4,16,16]{2,1,0:T(8,128)S(1)} copy-done((s32[4,16,16]{2,1,0:T(8,128)S(1)}, s32[4,16,16]{2,1,0:T(8,128)}, u32[]{:S(2)}) %copy-start.4) | copy-done | bytes 4120
  5.4 0.0 copy-start.5
  5.4 0.7 %copy-done.5 = s32[1,1,2,64]{3,2,1,0:T(2,128)S(1)} copy-done((s32[1,1,2,64]{3,2,1,0:T(2,128)S(1)}, s32[1,1,2,64]{3,2,1,0:T(2,128)}, u32[]{:S(2)}) %copy-start.5) | copy-done | bytes 536
  6.1 13.7 %shard_map.85 = (f32[16,16,128]{2,1,0:T(8,128)S(1)}, f32[16,16,128]{2,1,0:T(8,128)S(1)}, f32[16,16,128]{2,1,0:T(8,128)S(1)}) custom-call(f32[3,16,16,128]{3,2,1,0:T(8,128)S(1)} %copy-done.1, f32[16,16,128]{2,1,0:T(8,128)S(1)} %copy-done.2, f32[16,16,128]{2,1,0:T(8,128)S(1)} %copy-done.3, s32[1,1,2,64]{3,2,1,0:T(2,128)S(1)} %copy-done.5, ...), custom_call_target="tpu_custom_call" | custom-call | tf_op jit(solution)/shard_map/pallas_call | solution.py:271
  19.8 0.7 %copy.12 = f32[16,16,128]{2,1,0:T(8,128)} copy(f32[16,16,128]{2,1,0:T(8,128)S(1)} %get-tuple-element.6) | data formatting | bytes 262144
  20.4 0.7 %copy.13 = f32[16,16,128]{2,1,0:T(8,128)} copy(f32[16,16,128]{2,1,0:T(8,128)S(1)} %get-tuple-element.7) | data formatting | bytes 262144
  21.1 0.7 %copy.14 = f32[16,16,128]{2,1,0:T(8,128)} copy(f32[16,16,128]{2,1,0:T(8,128)S(1)} %get-tuple-element.8) | data formatting | bytes 262144
Async XLA Ops:
  0.6 1.2 %copy-start = (f32[8,16,16,128]{3,2,1,0:T(8,128)S(1)}, f32[8,16,16,128]{3,2,1,0:T(8,128)}, u32[]{:S(2)}) copy-start(f32[8,16,16,128]{3,2,1,0:T(8,128)} %weights_in.1) | copy-start | bytes 3145732
  1.9 1.0 %copy-start.1 = (f32[3,16,16,128]{3,2,1,0:T(8,128)S(1)}, f32[3,16,16,128]{3,2,1,0:T(8,128)}, u32[]{:S(2)}) copy-start(f32[3,16,16,128]{3,2,1,0:T(8,128)} %vel.1) | copy-start | bytes 1179652
  2.9 0.9 %copy-start.2 = (f32[16,16,128]{2,1,0:T(8,128)S(1)}, f32[16,16,128]{2,1,0:T(8,128)}, u32[]{:S(2)}) copy-start(f32[16,16,128]{2,1,0:T(8,128)} %lm_in.1) | copy-start | bytes 393220
  3.8 0.9 %copy-start.3 = (f32[16,16,128]{2,1,0:T(8,128)S(1)}, f32[16,16,128]{2,1,0:T(8,128)}, u32[]{:S(2)}) copy-start(f32[16,16,128]{2,1,0:T(8,128)} %mm_in.1) | copy-start | bytes 393220
  4.7 0.8 %copy-start.4 = (s32[4,16,16]{2,1,0:T(8,128)S(1)}, s32[4,16,16]{2,1,0:T(8,128)}, u32[]{:S(2)}) copy-start(s32[4,16,16]{2,1,0:T(8,128)} %slots_in.1) | copy-start | bytes 12292
  5.4 0.7 %copy-start.5 = (s32[1,1,2,64]{3,2,1,0:T(2,128)S(1)}, s32[1,1,2,64]{3,2,1,0:T(2,128)}, u32[]{:S(2)}) copy-start(s32[1,1,2,64]{3,2,1,0:T(2,128)} %ids.1) | copy-start | bytes 1540

commit v2 on v1

v2 whole, which is shorter than its diff:
```python
import jax
import jax.numpy as jnp
from jax import lax
from jax.experimental import pallas as pl
from jax.experimental.pallas import tpu as pltpu
from jax.sharding import PartitionSpec as P

pair_list = ((0, 0), (1, 1), (2, 2), (0, 1), (0, 2), (1, 2))
time_step = 0.75
floor_value = 0.3
directions = tuple((dx, dy) for dx in (-1, 0, 1) for dy in (-1, 0, 1) if (dx, dy) != (0, 0))
reach = 4
pad_y = 8
MESH = pl.DeviceIdType.MESH


def halves(table):
    high = table.astype(jnp.bfloat16)
    low = (table - high.astype(jnp.float32)).astype(jnp.bfloat16)
    return jnp.concatenate([high, low], axis=0)


def root(value):
    return value * lax.rsqrt(value)


def kernel(
    vel, lm_in, mm_in, ids, slots_in, weights_in, new_lm_out, new_mm_out, visc_out,
    u, lm, mm, slots, w, raw, lists, picked, far_picked, own_moved, raws, mags, smooth, outs,
    send_sems, recv_sems, local_sems, out_sems,
):
    nx, ny, nz = lm.shape
    groups, peers = lax.axis_size("age"), lax.axis_size("slab")
    g, s = lax.axis_index("age"), lax.axis_index("slab")

    def has(dx, dy):
        ok = jnp.bool_(True)
        if dx < 0:
            ok = ok & (g > 0)
        if dx > 0:
            ok = ok & (g < groups - 1)
        if dy < 0:
            ok = ok & (s > 0)
        if dy > 0:
            ok = ok & (s < peers - 1)
        return ok

    own_vel = pltpu.make_async_copy(
        vel, u.at[:, pl.ds(2, nx), pl.ds(pad_y, ny), :], local_sems.at[0]
    )
    own_copies = [
        pltpu.make_async_copy(slots_in, slots, local_sems.at[1]),
        pltpu.make_async_copy(lm_in, lm, local_sems.at[2]),
        pltpu.make_async_copy(mm_in, mm, local_sems.at[3]),
    ]
    weight_copy = pltpu.make_async_copy(weights_in, w, local_sems.at[4])

    barrier = pltpu.get_barrier_semaphore()
    for dx, dy in directions:
        @pl.when(has(dx, dy))
        def _(dx=dx, dy=dy):
            pl.semaphore_signal(barrier, inc=1, device_id=(g + dx, s + dy), device_id_type=MESH)

    for copy in own_copies:
        copy.start()
    own_vel.start()
    weight_copy.start()

    zero = jnp.zeros((), jnp.float32)
    for dx, place in ((-1, 0), (1, nx + 2)):
        @pl.when(jnp.logical_not(has(dx, 0)))
        def _(place=place):
            u[:, place : place + 2, :, :] = jnp.zeros((3, 2) + u.shape[2:], jnp.float32)
    for dy, place in ((-1, pad_y - 2), (1, pad_y + ny)):
        @pl.when(jnp.logical_not(has(0, dy)))
        def _(dy=dy, place=place):
            u[:, :, place : place + 2, :] = jnp.zeros(u.shape[:2] + (2, nz), jnp.float32)
            side = 0 if dy < 0 else 1
            raw[:, :, side * reach : (side + 1) * reach, :] = jnp.zeros((2, nx, reach, nz), jnp.float32)
            lists[side] = jnp.full(lists.shape[1:], -1, jnp.int32)

    def span(step, cells, begin):
        if step == 0:
            return pl.ds(0, cells), pl.ds(begin, cells)
        if step > 0:
            return pl.ds(cells - 2, 2), pl.ds(begin - 2, 2)
        return pl.ds(0, 2), pl.ds(begin + cells, 2)

    def remote(source, target, place, dx, dy):
        return pltpu.make_async_remote_copy(
            src_ref=source, dst_ref=target, send_sem=send_sems.at[place],
            recv_sem=recv_sems.at[place], device_id=(g + dx, s + dy), device_id_type=MESH,
        )

    halo = []
    for place, (dx, dy) in enumerate(directions):
        from_x, to_x = span(dx, nx, 2)
        from_y, to_y = span(dy, ny, pad_y)
        halo.append((
            dx, dy,
            remote(vel.at[:, from_x, from_y, :], u.at[:, to_x, to_y, :], place, dx, dy),
        ))
    memory = []
    place = len(directions)
    for dy in (1, -1):
        side = 0 if dy > 0 else 1
        columns = pl.ds(ny - reach, reach) if dy > 0 else pl.ds(0, reach)
        for number, field in enumerate((lm_in, mm_in)):
            memory.append((0, dy, remote(
                field.at[:, columns, :], raw.at[number, :, pl.ds(side * reach, reach), :], place, 0, dy
            )))
            place += 1
        memory.append((0, dy, remote(ids.at[0, 0], lists.at[side], place, 0, dy)))
        place += 1

    incoming = (
        ((g > 0).astype(jnp.int32) + (g < groups - 1).astype(jnp.int32) + 1)
        * ((s > 0).astype(jnp.int32) + (s < peers - 1).astype(jnp.int32) + 1)
        - 1
    )
    pl.semaphore_wait(barrier, incoming)
    for dx, dy, copy in halo + memory:
        @pl.when(has(dx, dy))
        def _(copy=copy):
            copy.start()

    for copy in own_copies:
        copy.wait()
    lines = 4 * nx
    blocks = nx * ny
    slot_rows = slots[...].astype(jnp.float32).reshape(lines, 1, ny)
    lane = lax.broadcasted_iota(jnp.int32, (1, ny, ny), 2)
    edge_row = lax.broadcasted_iota(jnp.int32, (1, 2 * reach, ny), 1)
    edge_row = jnp.where(edge_row < reach, edge_row, edge_row + ny - 2 * reach)

    def slot_column(wanted):
        picks = jnp.where(lane[:, : wanted.shape[1]] == wanted, slot_rows, 0.0)
        return jnp.sum(picks, axis=2, keepdims=True)

    def one_hot(column, begin, count):
        ids_of = (lax.broadcasted_iota(jnp.int32, (1, 1, count), 2) + begin).astype(jnp.float32)
        hot = jnp.where(column == ids_of, 1.0, 0.0)
        hot = hot.reshape(lines * column.shape[1], count).astype(jnp.bfloat16)
        return jnp.concatenate([hot, hot], axis=1)

    own_table = jnp.concatenate([lm[...].reshape(blocks, nz), mm[...].reshape(blocks, nz)], axis=1)
    own_hot = one_hot(slot_column(lax.broadcasted_iota(jnp.int32, (1, ny, ny), 1)), 0, blocks)
    picked[...] = jnp.dot(own_hot, halves(own_table), preferred_element_type=jnp.float32)
    capacity = lists.shape[2]
    far_hot = one_hot(slot_column(edge_row), blocks, 2 * capacity)
    weight_copy.wait()

    def own_step(x, carry):
        for half in range(ny // 8):
            moved = [None, None]
            for corner in range(4):
                low = w[2 * corner, x, half * 8 : half * 8 + 8, :]
                high = w[2 * corner + 1, x, half * 8 : half * 8 + 8, :]
                start = pl.multiple_of((corner * nx + x) * ny, ny) + half * 8
                for field in range(2):
                    base = picked[pl.ds(pl.multiple_of(start, 8), 8), field * nz : (field + 1) * nz]
                    term = low * base + high * pltpu.roll(base, nz - 1, 1)
                    moved[field] = term if moved[field] is None else moved[field] + term
            for field in range(2):
                own_moved[field, x, half * 8 : half * 8 + 8, :] = moved[field]
        return carry

    lax.fori_loop(0, nx, own_step, 0)

    own_vel.wait()
    for dx, dy, copy in halo:
        @pl.when(has(-dx, -dy))
        def _(copy=copy):
            copy.wait_recv()

    row = lax.broadcasted_iota(jnp.int32, (8, nz), 0)
    chunks = raws.shape[2] // 8
    insides = []
    for chunk in range(chunks):
        low = jnp.where((row + 8 * chunk > 0) | (s > 0), 1.0, 0.0)
        insides.append(jnp.where((row + 8 * chunk < ny + 1) | (s < peers - 1), low, 0.0))

    def strain_at(e, slot):
        shift = e // 1024
        within = jnp.where(((e > 0) | (g > 0)) & ((e < nx + 1) | (g < groups - 1)), 1.0, 0.0)
        def get(comp, along_x, along_y, count):
            return u[comp, e + 1 + along_x, pl.ds(pad_y - 1 + along_y + shift, count), :]
        for chunk in range(chunks):
            k = 8 * chunk
            center = [get(comp, 0, k, 8) for comp in range(3)]
            slopes = [
                [get(comp, 1, k, 8) - get(comp, -1, k, 8) for comp in range(3)],
                [get(comp, 0, k + 1, 8) - get(comp, 0, k - 1, 8) for comp in range(3)],
                [pltpu.roll(center[comp], nz - 1, 1) - pltpu.roll(center[comp], 1, 1) for comp in range(3)],
            ]
            mask = insides[chunk] * within
            parts = [(slopes[b][a] + slopes[a][b]) * mask for a, b in pair_list]
            total = parts[0] * parts[0] + parts[1] * parts[1] + parts[2] * parts[2]
            total = total + 2.0 * (parts[3] * parts[3] + parts[4] * parts[4] + parts[5] * parts[5])
            mag = root(total * 0.125 + 1e-06)
            mags[e, k : k + 8, :] = mag
            for place in range(6):
                a, b = pair_list[place]
                raws[slot, place, k : k + 8, :] = parts[place]
                raws[slot, 6 + place, k : k + 8, :] = mag * parts[place]
                raws[slot, 12 + place, k : k + 8, :] = center[a] * center[b]
        for place in range(18):
            below = raws[slot, place, pl.ds(shift, ny), :]
            middle = raws[slot, place, pl.ds(shift + 1, ny), :]
            above = raws[slot, place, pl.ds(shift + 2, ny), :]
            smooth[place, e] = (below + above) + (middle + middle)
        for comp in range(3):
            middle = get(comp, 0, 1, ny)
            smooth[18 + comp, e] = (get(comp, 0, 0, ny) + get(comp, 0, 2, ny)) + (middle + middle)

    def strain_step(i, carry):
        for slot in range(raws.shape[0]):
            strain_at(i * raws.shape[0] + slot, slot)
        return carry

    lax.fori_loop(0, (nx + 2) // raws.shape[0], strain_step, 0)

    for dx, dy, copy in memory:
        @pl.when(has(-dx, -dy))
        def _(copy=copy):
            copy.wait_recv()
    strip = nx * 2 * reach
    near = jnp.concatenate([raw[0].reshape(strip, nz), raw[1].reshape(strip, nz)], axis=1)
    near = halves(near)
    line = lax.broadcasted_iota(jnp.int32, (strip, capacity), 0)
    column = line % (2 * reach)
    line_row = line // (2 * reach)
    below_id = jnp.where(column < reach, line_row * ny + (ny - reach) + column, -5)
    above_id = jnp.where(column >= reach, line_row * ny + column - reach, -5)
    listed = []
    for side, block_id in ((0, below_id), (1, above_id)):
        hot = jnp.where(block_id == lists[side, side : side + 1, :], 1.0, 0.0).astype(jnp.bfloat16)
        hot = jnp.concatenate([hot, hot], axis=0)
        listed.append(lax.dot_general(hot, near, (((0,), (0,)), ((), ())), preferred_element_type=jnp.float32))
    far_table = halves(jnp.concatenate(listed, axis=0))
    far_picked[...] = jnp.dot(far_hot, far_table, preferred_element_type=jnp.float32)
    edge_low = lax.broadcasted_iota(jnp.int32, (8, nz), 0) < reach

    def final_step(x, carry):
        shift = x // 1024
        def filtered(half, place):
            ys = slice(half * 8, half * 8 + 8)
            f = (smooth[place, x, ys] + smooth[place, x + 2, ys]) + 2.0 * smooth[place, x + 1, ys]
            return (pltpu.roll(f, 1, 1) + pltpu.roll(f, nz - 1, 1)) + (f + f)
        far = [None, None]
        for corner in range(4):
            low = jnp.where(edge_low, w[2 * corner, x, 0:8, :], w[2 * corner, x, ny - 8 : ny, :])
            high = jnp.where(edge_low, w[2 * corner + 1, x, 0:8, :], w[2 * corner + 1, x, ny - 8 : ny, :])
            start = pl.multiple_of((corner * nx + x) * 8, 8)
            for field in range(2):
                base = far_picked[pl.ds(start, 8), field * nz : (field + 1) * nz]
                term = low * base + high * pltpu.roll(base, nz - 1, 1)
                far[field] = term if far[field] is None else far[field] + term
        for half in range(ny // 8):
            ys = slice(half * 8, half * 8 + 8)
            def keep(value):
                return jnp.where(edge_low, value, 0.0) if half == 0 else jnp.where(edge_low, 0.0, value)
            flow = [0.125 * filtered(half, 18 + comp) for comp in range(3)]
            parts = [filtered(half, place) for place in range(6)]
            total = parts[0] * parts[0] + parts[1] * parts[1] + parts[2] * parts[2]
            total = total + 2.0 * (parts[3] * parts[3] + parts[4] * parts[4] + parts[5] * parts[5])
            mag4 = 4.0 * root(total * (2.0 / 65536.0) + 1e-06)
            lm_sum, mm_sum = [], []
            for group in (range(3), range(3, 6)):
                lm_part = mm_part = None
                for place in group:
                    a, b = pair_list[place]
                    leonard = filtered(half, 12 + place) - flow[a] * flow[b]
                    model = filtered(half, 6 + place) - mag4 * parts[place]
                    lm_part = leonard * model if lm_part is None else lm_part + leonard * model
                    mm_part = model * model if mm_part is None else mm_part + model * model
                lm_sum.append(lm_part)
                mm_sum.append(mm_part)
            lm_local = (lm_sum[0] + 2.0 * lm_sum[1]) * (1.0 / 8192.0)
            mm_local = (mm_sum[0] + 2.0 * mm_sum[1]) * (1.0 / 16384.0)
            moved_lm = own_moved[0, x, ys, :] + keep(far[0])
            moved_mm = own_moved[1, x, ys, :] + keep(far[1])
            power = root(root(root(jnp.maximum(jnp.maximum(moved_lm, 0.0) * moved_mm, floor_value))))
            rate = (time_step / 1.5) * power
            blend = rate / (1.0 + rate)
            new_lm = jnp.maximum(moved_lm + blend * (lm_local - moved_lm), 0.0)
            new_mm = moved_mm + blend * (mm_local - moved_mm)
            outs[0, x, ys, :] = new_lm
            outs[1, x, ys, :] = new_mm
            outs[2, x, ys, :] = new_lm / new_mm * mags[x + 1, pl.ds(half * 8 + 1 + shift, 8), :]
        return carry

    sent = []
    unroll = nx // 2
    for part in range(2):
        strip_x = pl.ds(part * (nx // 2), nx // 2)
        lax.fori_loop(part * (nx // 2), (part + 1) * (nx // 2), final_step, 0, unroll=unroll)
        for place, target in enumerate((new_lm_out, new_mm_out, visc_out)):
            copy = pltpu.make_async_copy(outs.at[place, strip_x], target.at[strip_x], out_sems.at[part, place])
            copy.start()
            sent.append(copy)

    for dx, dy, copy in halo + memory:
        @pl.when(has(dx, dy))
        def _(copy=copy):
            copy.wait_send()
    for copy in sent:
        copy.wait()


def hand_over(a_in, b_in, c_in, a_out, b_out, c_out):
    a_out[...] = a_in[...]
    b_out[...] = b_in[...]
    c_out[...] = c_in[...]


def on_device(velocity, mem_lm, mem_mm, send_ids, read_slot, weights):
    nx, ny, nz = mem_lm.shape
    capacity = send_ids.shape[3]
    f32 = jnp.float32
    rows = ny + 8
    out = jax.ShapeDtypeStruct(mem_lm.shape, f32)
    copies = len(directions) + 6
    fields = pl.pallas_call(
        kernel,
        out_shape=(out, out, out),
        in_specs=[pl.BlockSpec(memory_space=pltpu.HBM)] * 6,
        out_specs=[pl.BlockSpec(memory_space=pltpu.HBM)] * 3,
        scratch_shapes=[
            pltpu.VMEM((3, nx + 4, ny + 2 * pad_y, nz), f32),
            pltpu.VMEM(mem_lm.shape, f32),
            pltpu.VMEM(mem_lm.shape, f32),
            pltpu.VMEM(read_slot.shape, jnp.int32),
            pltpu.VMEM(weights.shape, f32),
            pltpu.VMEM((2, nx, 2 * reach, nz), f32),
            pltpu.VMEM((2, 2, capacity), jnp.int32),
            pltpu.VMEM((4 * nx * ny, 2 * nz), f32),
            pltpu.VMEM((4 * nx * 2 * reach, 2 * nz), f32),
            pltpu.VMEM((2,) + mem_lm.shape, f32),
            pltpu.VMEM((3, 18, rows, nz), f32),
            pltpu.VMEM((nx + 2, rows, nz), f32),
            pltpu.VMEM((21, nx + 2, ny, nz), f32),
            pltpu.VMEM((3,) + mem_lm.shape, f32),
            pltpu.SemaphoreType.DMA((copies,)),
            pltpu.SemaphoreType.DMA((copies,)),
            pltpu.SemaphoreType.DMA((5,)),
            pltpu.SemaphoreType.DMA((2, 3)),
        ],
        compiler_params=pltpu.CompilerParams(
            collective_id=0, has_side_effects=True, vmem_limit_bytes=60 << 20
        ),
    )(velocity, mem_lm, mem_mm, send_ids, read_slot, weights)
    return pl.pallas_call(
        hand_over,
        out_shape=(out, out, out),
        in_specs=[pl.BlockSpec(memory_space=pltpu.VMEM)] * 3,
        out_specs=[pl.BlockSpec(memory_space=pltpu.VMEM)] * 3,
        compiler_params=pltpu.CompilerParams(vmem_limit_bytes=60 << 20),
    )(*fields)


def solution(mesh):
    return jax.shard_map(
        on_device,
        mesh=mesh,
        in_specs=(
            P(None, "age", "slab", None),
            P("age", "slab", None),
            P("age", "slab", None),
            P("age", "slab", None, None),
            P(None, "age", "slab"),
            P(None, "age", "slab", None),
        ),
        out_specs=(P("age", "slab", None), P("age", "slab", None), P("age", "slab", None)),
        check_vma=False,
    )
```

time: 22.1 us -> 13.9 us (0.63)
  local copies, waits for them, and re-layouts: 7.42 us -> 0 us
  Pallas kernels: 13.7 us -> 13.1 us
    unnamed x15 -> x0, local copies, waits for them, and re-layouts: 7.42 us -> none
    pallas_call x1, Pallas kernels: 13.7 us -> 11.3 us  [on_device(): pl.pallas_call(kernel, out_shape=(out, out, out), in_specs=[pl.BlockSpec(...]
    pallas_call x0 -> x1, Pallas kernels: none -> 1.78 us  [on_device(): pl.pallas_call(hand_over, out_shape=(out, out, out), in_specs=[pl.BlockSp...]
where the time goes in v2:
time: 13.9 us; the launch traced here: 13.7 us
  Pallas kernels  13.1 us (94%)
  between operations  0.64 us (5%)
    pallas_call x1, Pallas kernels, on_device(): pl.pallas_call(kernel, out_shape=(out, out, out), in_specs=[pl.BlockSpec(...  11.3 us
    pallas_call x1, Pallas kernels, on_device(): pl.pallas_call(hand_over, out_shape=(out, out, out), in_specs=[pl.BlockSp...  1.78 us

profile of v2, /device:TPU:12, one launch (start us, length us, event | category | flops | bytes accessed | tf_op | source)
XLA Modules:
  0.0 13.7 jit_solution(3852316382000500625)
XLA Ops:
  0.6 11.3 %shard_map.85 = (f32[16,16,128]{2,1,0:T(8,128)}, f32[16,16,128]{2,1,0:T(8,128)}, f32[16,16,128]{2,1,0:T(8,128)}) custom-call(f32[3,16,16,128]{3,2,1,0:T(8,128)} %vel.1, f32[16,16,128]{2,1,0:T(8,128)} %lm_in.1, f32[16,16,128]{2,1,0:T(8,128)} %mm_in.1, s32[1,1,2,64]{3,2,1,0:T(2,128)} %ids.1, s32[4,16,16]{2,1,0:T(8,128)} %slots_in.1, f32[8,16,16,128]{3,2,1,0:T(8,128)} %weights_in.1), custom_call_target="tpu_custom_call" | custom-call | tf_op jit(solution)/shard_map/pallas_call | solution.py:324
  11.9 1.8 %shard_map.86 = (f32[16,16,128]{2,1,0:T(8,128)}, f32[16,16,128]{2,1,0:T(8,128)}, f32[16,16,128]{2,1,0:T(8,128)}) custom-call(f32[16,16,128]{2,1,0:T(8,128)} %get-tuple-element.6.a_in, f32[16,16,128]{2,1,0:T(8,128)} %get-tuple-element.7.b_in, f32[16,16,128]{2,1,0:T(8,128)} %get-tuple-element.8.c_in), custom_call_target="tpu_custom_call" | custom-call | tf_op jit(solution)/shard_map/pallas_call | solution.py:353

commit v3 on v2

--- a/solution.py
+++ b/solution.py
@@ -308,10 +308,18 @@
         copy.wait()
 
 
-def hand_over(a_in, b_in, c_in, a_out, b_out, c_out):
-    a_out[...] = a_in[...]
-    b_out[...] = b_in[...]
-    c_out[...] = c_in[...]
+def hand_over(a_in, b_in, c_in, a_out, b_out, c_out, held, in_sems, out_sems):
+    arrivals, departures = [], []
+    for place, (source, target) in enumerate(((a_in, a_out), (b_in, b_out), (c_in, c_out))):
+        arrivals.append(pltpu.make_async_copy(source, held.at[place], in_sems.at[place]))
+        departures.append(pltpu.make_async_copy(held.at[place], target, out_sems.at[place]))
+    for copy in arrivals:
+        copy.start()
+    for arrival, departure in zip(arrivals, departures):
+        arrival.wait()
+        departure.start()
+    for copy in departures:
+        copy.wait()
 
 
 def on_device(velocity, mem_lm, mem_mm, send_ids, read_slot, weights):
@@ -337,7 +345,7 @@
             pltpu.VMEM((4 * nx * ny, 2 * nz), f32),
             pltpu.VMEM((4 * nx * 2 * reach, 2 * nz), f32),
             pltpu.VMEM((2,) + mem_lm.shape, f32),
-            pltpu.VMEM((3, 18, rows, nz), f32),
+            pltpu.VMEM((6, 18, rows, nz), f32),
             pltpu.VMEM((nx + 2, rows, nz), f32),
             pltpu.VMEM((21, nx + 2, ny, nz), f32),
             pltpu.VMEM((3,) + mem_lm.shape, f32),
@@ -353,8 +361,13 @@
     return pl.pallas_call(
         hand_over,
         out_shape=(out, out, out),
-        in_specs=[pl.BlockSpec(memory_space=pltpu.VMEM)] * 3,
-        out_specs=[pl.BlockSpec(memory_space=pltpu.VMEM)] * 3,
+        in_specs=[pl.BlockSpec(memory_space=pltpu.HBM)] * 3,
+        out_specs=[pl.BlockSpec(memory_space=pltpu.HBM)] * 3,
+        scratch_shapes=[
+            pltpu.VMEM((3,) + mem_lm.shape, f32),
+            pltpu.SemaphoreType.DMA((3,)),
+            pltpu.SemaphoreType.DMA((3,)),
+        ],
         compiler_params=pltpu.CompilerParams(vmem_limit_bytes=60 << 20),
     )(*fields)
 

time: 13.9 us -> 13.6 us (0.978)
  Pallas kernels: 13.1 us -> 12.8 us
    pallas_call x1, Pallas kernels: 11.3 us -> 11.1 us  [on_device(): pl.pallas_call(kernel, out_shape=(out, out, out), in_specs=[pl.BlockSpec(...]
where the time goes in v3:
time: 13.6 us; the launch traced here: 13.5 us
  Pallas kernels  12.8 us (94%)
  between operations  0.64 us (5%)
    pallas_call x1, Pallas kernels, on_device(): pl.pallas_call(kernel, out_shape=(out, out, out), in_specs=[pl.BlockSpec(...  11.1 us
    pallas_call x1, Pallas kernels, on_device(): pl.pallas_call(hand_over, out_shape=(out, out, out), in_specs=[pl.BlockSp...  1.74 us

profile of v3, /device:TPU:12, one launch (start us, length us, event | category | flops | bytes accessed | tf_op | source)
XLA Modules:
  0.0 13.5 jit_solution(2356528468844832981)
XLA Ops:
  0.6 11.1 %shard_map.85 = (f32[16,16,128]{2,1,0:T(8,128)}, f32[16,16,128]{2,1,0:T(8,128)}, f32[16,16,128]{2,1,0:T(8,128)}) custom-call(f32[3,16,16,128]{3,2,1,0:T(8,128)} %vel.1, f32[16,16,128]{2,1,0:T(8,128)} %lm_in.1, f32[16,16,128]{2,1,0:T(8,128)} %mm_in.1, s32[1,1,2,64]{3,2,1,0:T(2,128)} %ids.1, s32[4,16,16]{2,1,0:T(8,128)} %slots_in.1, f32[8,16,16,128]{3,2,1,0:T(8,128)} %weights_in.1), custom_call_target="tpu_custom_call" | custom-call | tf_op jit(solution)/shard_map/pallas_call | solution.py:332
  11.7 1.7 %shard_map.86 = (f32[16,16,128]{2,1,0:T(8,128)}, f32[16,16,128]{2,1,0:T(8,128)}, f32[16,16,128]{2,1,0:T(8,128)}) custom-call(f32[16,16,128]{2,1,0:T(8,128)} %get-tuple-element.6.a_in, f32[16,16,128]{2,1,0:T(8,128)} %get-tuple-element.7.b_in, f32[16,16,128]{2,1,0:T(8,128)} %get-tuple-element.8.c_in), custom_call_target="tpu_custom_call" | custom-call | tf_op jit(solution)/shard_map/pallas_call | solution.py:361
